TPU v7x, 32 devices: a whole 2x2x4 slice. The times are simulated.
32 devices in a mesh: col: 4 (over y, core), row: 4 (over z), tok: 2 (over x).
Axes of the slice: x: 2, y: 2, z: 4, core: 2. Of those that a mesh axis runs over, the one named last changes fastest.
Arguments:
- queries: bfloat16 [256, 16384], P('tok', ('col', 'row')), may hold values from -512 to 512
- key_rows: bfloat16 [256, 16384], P('tok', ('col', 'row')), may hold values from -12 to 12
- values: bfloat16 [256, 16384], P('tok', ('col', 'row')), may hold values from -6 to 6
- code_first: int32 [16384, 2048], P(('row', 'tok'), 'col'), may hold values from 0 to 255
- code_second: int32 [16384, 2048], P(('row', 'tok'), 'col'), may hold values from 0 to 255
- book_first: bfloat16 [256, 8], replicated, may hold values from -0.59765625 to 0.59765625
- book_second: bfloat16 [256, 8], replicated, may hold values from -0.59765625 to 0.59765625
- scales: float32 [16384], P(('row', 'tok')), may hold values from 0.015 to 0.15
- target: bfloat16 [256, 16384], P(None, ('row', 'tok')), may hold values from -2 to 2
Outputs:
- misfit: bfloat16 [256, 16384], P(None, ('row', 'tok'))
- grad_scales: float32 [16384], P(('row', 'tok'))
- grad_books: float32 [2, 256, 8], replicated
All inputs are finite; a program needn't handle non-finite values.
Results may differ from a plain program's by a relative error of at most 0.0053.
Values may be sent and summed in bfloat16 or wider, within the bound.
A program may use at most 128 MiB of HBM per device.

v0:
```python
import math

import jax
import jax.numpy as jnp
from jax import lax
from jax.sharding import PartitionSpec as P

HEAD_DIM = 128
ENTRIES = 256
GROUP = 8


def one_hot_codes(codes):
    return (codes[..., None] == lax.iota(jnp.int32, ENTRIES)).astype(jnp.bfloat16)


def dequantize(first_codes, second_codes, book_first, book_second):
    rows, groups = first_codes.shape
    first_part = jnp.einsum(
        "rgk,kj->rgj", one_hot_codes(first_codes), book_first, preferred_element_type=jnp.float32
    )
    second_part = jnp.einsum(
        "rgk,kj->rgj", one_hot_codes(second_codes), book_second, preferred_element_type=jnp.float32
    )
    return (first_part + second_part).reshape(rows, groups * GROUP)


def split_terms(scaled):
    upper = scaled.astype(jnp.bfloat16)
    lower = (scaled - upper.astype(jnp.float32)).astype(jnp.bfloat16)
    return jnp.concatenate([upper, lower], axis=-1)


def bin_terms(codes, split):
    parts = jnp.einsum(
        "rgk,rgj->kj", one_hot_codes(codes), split, preferred_element_type=jnp.float32
    )
    return parts[:, :GROUP] + parts[:, GROUP:]


def block_size(rows, groups):
    return math.gcd(rows, max(1, 32768 // groups))


def tile_unscaled(code_first, code_second, book_first, book_second):
    rows, groups = code_first.shape
    block = block_size(rows, groups)
    count = rows // block

    def one_block(operands):
        first_codes, second_codes = operands
        return dequantize(first_codes, second_codes, book_first, book_second)

    blocks = lax.map(
        one_block,
        (code_first.reshape(count, block, groups), code_second.reshape(count, block, groups)),
    )
    return blocks.reshape(rows, groups * GROUP)


def tile_grads(code_first, code_second, scales, unscaled_rows, grad_rows):
    rows, groups = code_first.shape
    block = block_size(rows, groups)
    count = rows // block

    def step(total, index):
        start = index * block
        first_codes = lax.dynamic_slice_in_dim(code_first, start, block, 0)
        second_codes = lax.dynamic_slice_in_dim(code_second, start, block, 0)
        row_scales = lax.dynamic_slice_in_dim(scales, start, block, 0)
        unscaled = unscaled_rows(first_codes, second_codes, start, block)
        weight_grad = grad_rows(start, block)
        scale_part = jnp.sum(weight_grad * unscaled, axis=1)
        split = split_terms((row_scales[:, None] * weight_grad).reshape(block, groups, GROUP))
        total = total + jnp.stack([bin_terms(first_codes, split), bin_terms(second_codes, split)])
        return (total, scale_part)

    total, parts = lax.scan(
        step, jnp.zeros((2, ENTRIES, GROUP), jnp.float32), lax.iota(jnp.int32, count)
    )
    return (total, parts.reshape(rows))


def local(
    queries, key_rows, values, code_first, code_second, book_first, book_second, scales, target
):
    tok_rows, width = queries.shape
    heads_here = width // HEAD_DIM
    query_heads = queries.reshape(tok_rows, heads_here, HEAD_DIM)
    query_place = lax.axis_index("tok") * tok_rows + lax.iota(jnp.int32, tok_rows)
    running_max = jnp.full((heads_here, tok_rows), -1e30, jnp.float32)
    key_piece = lax.all_gather(key_rows, "tok", axis=0, tiled=True)
    value_piece = lax.all_gather(values, "tok", axis=0, tiled=True)
    length = key_piece.shape[0]
    key_heads = key_piece.reshape(length, heads_here, HEAD_DIM)
    value_heads = value_piece.reshape(length, heads_here, HEAD_DIM)
    scores = jnp.einsum(
        "qhd,khd->hqk", query_heads, key_heads, preferred_element_type=jnp.float32
    ) / math.sqrt(HEAD_DIM)
    key_place = lax.iota(jnp.int32, length)
    allowed = (key_place[None, :] <= query_place[:, None])[None]
    masked = jnp.where(allowed, scores, -1e30)
    fresh_max = jnp.maximum(running_max, jnp.max(masked, axis=-1))
    exponent = jnp.where(allowed, jnp.exp(scores - fresh_max[..., None]), 0.0)
    probs = exponent.astype(jnp.bfloat16)
    running_sum = jnp.sum(exponent, axis=-1)
    weighted = jnp.einsum("hqk,khd->hqd", probs, value_heads, preferred_element_type=jnp.float32)
    running_max, running_sum, weighted = (fresh_max, running_sum, weighted)
    attended = (
        (weighted / running_sum[..., None])
        .transpose(1, 0, 2)
        .reshape(tok_rows, width)
        .astype(jnp.bfloat16)
    )
    unscaled = tile_unscaled(code_first, code_second, book_first, book_second)
    weight = (scales[:, None] * unscaled).astype(jnp.bfloat16)
    head_cols = lax.all_gather(attended, "row", axis=1, tiled=True)
    gathered = lax.all_gather(head_cols, "tok", axis=0, tiled=True)
    partial_value = lax.dot_general(
        gathered, weight, (((1,), (1,)), ((), ())), preferred_element_type=jnp.float32
    )
    summed_out = lax.psum(partial_value, "col")
    misfit = (summed_out - target.astype(jnp.float32)).astype(jnp.bfloat16)
    token_count = misfit.shape[0]

    def grad_rows(start, size):
        misfit_cols = lax.dynamic_slice_in_dim(misfit, start, size, 1)
        return (
            lax.dot_general(
                misfit_cols, gathered, (((0,), (0,)), ((), ())), preferred_element_type=jnp.float32
            )
            / token_count
        )

    def stored_rows(first_codes, second_codes, start, size):
        return lax.dynamic_slice_in_dim(unscaled, start, size, 0)

    book_part, scale_part = tile_grads(code_first, code_second, scales, stored_rows, grad_rows)
    grad_scales = lax.psum(scale_part, "col")
    grad_books = lax.psum(book_part, ("col", "row", "tok"))
    return (misfit, grad_scales, grad_books)


def solution(mesh):
    in_specs = (
        P("tok", ("col", "row")),
        P("tok", ("col", "row")),
        P("tok", ("col", "row")),
        P(("row", "tok"), "col"),
        P(("row", "tok"), "col"),
        P(),
        P(),
        P(("row", "tok")),
        P(None, ("row", "tok")),
    )
    out_specs = (P(None, ("row", "tok")), P(("row", "tok")), P())
    return jax.shard_map(local, mesh=mesh, in_specs=in_specs, out_specs=out_specs, check_vma=False)
```

profile of v0, /device:TPU:0, one launch (start us, length us, event | category | flops | bytes accessed | tf_op | source)
XLA Modules:
  0.0 2325.3 jit_solution(10799589319663155681)
XLA Ops:
  29.2 29.3 %all-gather.3.cloned.1.call-done = bf16[128,4096]{1,0:T(8,128)(2,1)} async-done(((bf16[128,1024]{1,0:T(8,128)(2,1)}), bf16[128,4096]{1,0:T(8,128)(2,1)}) %all-gather.3.cloned.1.call-update) | async-done | bytes 1048592 | tf_op jit(solution)/shard_map/all_gather | solution.py:117
  58.5 832.4 %while.23 = (s32[]{:T(128)}, f32[32,64,4096]{2,1,0:T(8,128)}, s32[32,64,512]{2,1,0:T(8,128)}, bf16[256,8]{0,1:T(8,128)(2,1)S(1)}, s32[32,64,512]{2,1,0:T(8,128)}, /*index=5*/bf16[256,8]{0,1:T(8,128)(2,1)S(1)}, s32[]{:T(128)}) while((s32[]{:T(128)}, f32[32,64,4096]{2,1,0:T(8,128)}, s32[32,64,512]{2,1,0:T(8,128)}, bf16[256,8]{0,1:T(8,128)(2,1)S(1)}, ...), condition=%wide.region_3.4_spmd, body=%wide.region_2.3_spmd.sunk | while | flops 285474816 | bytes 10232401 | solution.py:54
  906.1 51.0 %all-reduce.2.cloned.1.call-done = f32[256,2048]{1,0:T(8,128)} async-done(((f32[256,2048]{1,0:T(8,128)}), f32[256,2048]{1,0:T(8,128)}) %all-reduce.2.cloned.1.call-update) | async-done | bytes 2097168 | tf_op jit(solution)/shard_map/psum | solution.py:122
  959.9 1311.9 %while.24 = (s32[]{:T(128)}, f32[2,256,8]{1,2,0:T(8,128)S(1)}, f32[32,64]{1,0:T(8,128)S(1)}, s32[32]{0:T(128)S(1)}, s32[2048,512]{1,0:T(8,128)}, /*index=5*/bf16...) while((s32[]{:T(128)}, f32[2,256,8]{1,2,0:T(8,128)S(1)}, ...), condition=%wide.region_7.8_spmd.clone, body=%wide.region_5.7_spmd.clone.sunk | while | flops 694173696 | bytes 21957368 | solution.py:78
  966.2 17.3 fusion.57
  983.5 17.3 fusion.55
  1007.2 17.3 fusion.57
  1024.5 17.3 fusion.55
  1048.2 17.3 fusion.57
  1065.5 17.3 fusion.55
  1089.2 17.3 fusion.57
  1106.5 17.3 fusion.55
  1130.2 17.3 fusion.57
  1147.5 17.3 fusion.55
  1171.2 17.3 fusion.57
  1188.5 17.3 fusion.55
  1212.2 17.3 fusion.57
  1229.5 17.3 fusion.55
  1253.2 17.3 fusion.57
  1294.2 17.3 fusion.57
  1311.5 17.3 fusion.55
  1352.5 17.3 fusion.55
  1622.1 17.3 fusion.57
  1827.1 17.3 fusion.57
  1844.5 17.3 fusion.55
  2049.4 17.3 fusion.55
  2073.1 17.3 fusion.57
  2090.4 17.3 fusion.55
  2155.1 17.3 fusion.57
  2196.1 17.3 fusion.57
  2213.4 17.3 fusion.55
  2278.3 40.4 %psum.23 = f32[2,256,8]{1,2,0:T(8,128)} all-reduce(f32[2,256,8]{1,2,0:T(8,128)S(1)} %get-tuple-element.348), channel_id=1, replica_groups=mesh['col'=4,'row'=4,'tok'=2] {'col','row','tok'}, use_global_device_ids=true, to_apply=%region_9.10 | all-reduce | flops 4096 | bytes 32768 | tf_op jit(solution)/shard_map/psum | solution.py:140
  (683 shorter events, 1698.8 us)
Async XLA Ops:
  7.2 51.3 %copy-start.5 = (bf16[256,8]{0,1:T(8,128)(2,1)S(1)}, bf16[256,8]{0,1:T(8,128)(2,1)}, u32[]{:S(2)}) copy-start(bf16[256,8]{0,1:T(8,128)(2,1)} %param.18) | copy-start | bytes 12292
  7.2 51.3 %copy-start.6 = (bf16[256,8]{0,1:T(8,128)(2,1)S(1)}, bf16[256,8]{0,1:T(8,128)(2,1)}, u32[]{:S(2)}) copy-start(bf16[256,8]{0,1:T(8,128)(2,1)} %param.19) | copy-start | bytes 12292
  7.2 51.2 %all-gather.3.cloned.1.call-start = ((), (), s32[]{:S(2)}) async-start(), calls=%async_computation | async-start | bytes 1310720 | tf_op jit(solution)/shard_map/all_gather | solution.py:117
  29.1 861.8 %all-gather.5.cloned.1.call-start = ((), (), s32[]{:S(2)}) async-start(), calls=%async_computation.1 | async-start | bytes 3145728 | tf_op jit(solution)/shard_map/all_gather | solution.py:118
  58.4 898.6 %all-reduce.2.cloned.1.call-start = ((), (), s32[]{:S(2)}) async-start(), calls=%async_computation.2 | async-start | bytes 4194304 | tf_op jit(solution)/shard_map/psum | solution.py:122
  58.5 832.4 %copy-start.4 = (f32[2048]{0:T(1024)S(1)}, f32[2048]{0:T(1024)}, u32[]{:S(2)}) copy-start(f32[2048]{0:T(1024)} %param.20) | copy-start | bytes 24580
  890.9 66.2 %copy-start.3 = (bf16[256,2048]{1,0:T(8,128)(2,1)S(1)}, bf16[256,2048]{1,0:T(8,128)(2,1)}, u32[]{:S(2)}) copy-start(bf16[256,2048]{1,0:T(8,128)(2,1)} %param.21) | copy-start | bytes 3145732
  890.9 69.0 %copy-start.1 = (bf16[256,4096]{1,0:T(8,128)(2,1)S(1)}, bf16[256,4096]{1,0:T(8,128)(2,1)}, u32[]{:S(2)}) copy-start(bf16[256,4096]{1,0:T(8,128)(2,1)} %all-gather.5.cloned.1.call-done) | copy-start | bytes 6291460
  983.5 17.4 copy-start.2
  1024.5 17.4 copy-start.2
  1065.5 17.4 copy-start.2
  1106.5 17.4 copy-start.2
  1147.5 17.4 copy-start.2
  1188.5 17.4 copy-start.2
  1270.5 17.4 copy-start.2
  1311.5 17.4 copy-start.2
  1352.5 17.4 copy-start.2
  1393.5 17.4 copy-start.2
  1475.5 17.4 copy-start.2
  1516.5 17.4 copy-start.2
  1557.5 17.4 copy-start.2
  1598.5 17.4 copy-start.2
  1639.5 17.4 copy-start.2
  1721.5 17.4 copy-start.2
  1844.4 17.4 copy-start.2
  1885.4 17.4 copy-start.2
  2008.4 17.4 copy-start.2
  2049.4 17.4 copy-start.2
  2090.4 17.4 copy-start.2
  2172.4 17.4 copy-start.2
  2213.4 17.4 copy-start.2
  2254.4 17.4 copy-start.2
  (9 other events, 150.5 us)
Sparse Core Ops, SparseCore 0:
  29.2 29.1 all-gather.2
  60.0 32.7 all-gather.4
  906.2 50.8 all-reduce.1
where the time goes:
time: 2330 us
  matrix products  1900 us (82%)
  local copies, waits for them, and re-layouts  232 us (10%)
  waiting for transfers between devices  80.3 us (3%)
  blocking collectives  65.2 us (3%)
  loops' own time  24.5 us (1%)
    dot_general x64, matrix products, bin_terms(): jnp.einsum('rgk,rgj->kj', one_hot_codes(codes), split, preferred_element_...  1110 us
    dot_general x32, matrix products, dequantize(): jnp.einsum('rgk,kj->rgj', one_hot_codes(second_codes), book_second, prefe...  356 us
    dot_general x32, matrix products, dequantize(): jnp.einsum('rgk,kj->rgj', one_hot_codes(first_codes), book_first, preferr...  355 us
    dot_general x32, matrix products, grad_rows(): lax.dot_general(misfit_cols, gathered, (((0,), (0,)), ((), ())), preferre...  63.4 us
    dynamic_update_slice x64, local copies, waits for them, and re-layouts, tile_unscaled(): lax.map(one_block, (code_first.reshape(count, block, groups), code_second...  53.1 us
    psum x1, waiting for transfers between devices, local(): summed_out = lax.psum(partial_value, 'col')  51 us
  transfers between devices with their start and end apart: 3, of which 2 were waited for; matrix products, arithmetic and copies ran while one was open for 36% of the time, Pallas kernels for 0%

commit v1 on v0

v1 whole, which is shorter than its diff:
```python
import functools
import math

import jax
import jax.numpy as jnp
from jax import lax
from jax.experimental import pallas as pl
from jax.experimental.pallas import tpu as pltpu
from jax.sharding import PartitionSpec as P

HEAD_DIM = 128
ENTRIES = 256
GROUP = 8
LANES = 128
LOW = 8
HIGH = ENTRIES // LOW
OCTET = 8
VMEM_LIMIT = 48 * 1024 * 1024


def look_up(table, codes):
    place = codes & (LANES - 1)
    lower = jnp.take_along_axis(table[0], place, axis=1, mode="promise_in_bounds")
    upper = jnp.take_along_axis(table[1], place, axis=1, mode="promise_in_bounds")
    return jnp.where((codes & LANES) != 0, upper, lower)


def dequantize_kernel(first_ref, second_ref, books_ref, scales_ref, weight_ref, codes_ref):
    codes_ref[...] = (first_ref[...] + second_ref[...] * ENTRIES).T
    groups, rows = codes_ref.shape
    tables = [
        [books_ref[book, :, half * LANES : (half + 1) * LANES] for half in range(2)]
        for book in range(2)
    ]

    @pl.loop(0, groups // 2, unroll=4)
    def _(pair):
        parts = []
        for side in range(2):
            row = codes_ref[pl.ds(pair * 2 + side, 1), :]
            pieces = []
            for start in range(0, rows, LANES):
                codes = jnp.broadcast_to(row[:, start : start + LANES], (GROUP, LANES))
                unscaled = look_up(tables[0], codes) + look_up(tables[1], codes >> 8)
                pieces.append(unscaled * scales_ref[:, start : start + LANES])
            parts.append(jnp.concatenate(pieces, axis=1))
        rows16 = pl.ds(pl.multiple_of(pair * 16, 16), 16)
        weight_ref[rows16, :] = jnp.concatenate(parts, axis=0).astype(jnp.bfloat16)


def dequantize(code_first, code_second, books, scales):
    rows, groups = code_first.shape
    block = math.gcd(rows, 512)
    return pl.pallas_call(
        dequantize_kernel,
        grid=(groups // LANES, rows // block),
        in_specs=[
            pl.BlockSpec((block, LANES), lambda g, o: (o, g)),
            pl.BlockSpec((block, LANES), lambda g, o: (o, g)),
            pl.BlockSpec((2, GROUP, ENTRIES), lambda g, o: (0, 0, 0)),
            pl.BlockSpec((1, block), lambda g, o: (0, o)),
        ],
        out_specs=[
            pl.BlockSpec((LANES * GROUP, block), lambda g, o: (g, o)),
            pl.BlockSpec((LANES, block), lambda g, o: (g, o)),
        ],
        out_shape=[
            jax.ShapeDtypeStruct((groups * GROUP, rows), jnp.bfloat16),
            jax.ShapeDtypeStruct((groups, rows), jnp.int32),
        ],
        compiler_params=pltpu.CompilerParams(vmem_limit_bytes=VMEM_LIMIT),
        cost_estimate=pl.CostEstimate(
            flops=32 * rows * groups * GROUP,
            bytes_accessed=rows * groups * (12 + 2 * GROUP),
            transcendentals=0,
        ),
        name="dequantize",
    )(code_first, code_second, books, scales)


def bin_kernel(chunk, attended_ref, misfit_ref, codes_ref, scales_ref, total_ref, grad_ref):
    @pl.when(pl.program_id(0) == 0)
    def _():
        total_ref[...] = jnp.zeros_like(total_ref)

    rows = misfit_ref.shape[1]
    groups = codes_ref.shape[0]
    width = OCTET * GROUP

    @pl.loop(0, rows // chunk)
    def _(part):
        cols = pl.ds(pl.multiple_of(part * chunk, chunk), chunk)
        grad_ref[...] = (
            jnp.dot(
                attended_ref[...], misfit_ref[:, cols], preferred_element_type=jnp.float32
            )
            * scales_ref[:, cols]
        ).astype(jnp.bfloat16)

        @pl.loop(0, groups // OCTET, unroll=2)
        def _(octet):
            grad = grad_ref[pl.ds(pl.multiple_of(octet * width, width), width), :]
            places = lax.broadcasted_iota(jnp.int32, (HIGH, chunk), 0).astype(jnp.bfloat16)
            lines = [codes_ref[pl.ds(octet * OCTET + g, 1), cols] for g in range(OCTET)]
            for book in range(2):
                own = [(line >> (8 * book)) & (ENTRIES - 1) for line in lines]
                low = jnp.concatenate(
                    [jnp.broadcast_to(code & (LOW - 1), (GROUP, chunk)) for code in own], axis=0
                ).astype(jnp.bfloat16)
                left = jnp.concatenate(
                    [
                        jnp.where(low == jnp.bfloat16(k), grad, jnp.bfloat16(0))
                        for k in range(LOW)
                    ],
                    axis=0,
                )
                right = jnp.concatenate(
                    [
                        jnp.where(
                            jnp.broadcast_to(code // LOW, (HIGH, chunk)).astype(jnp.bfloat16)
                            == places,
                            jnp.bfloat16(1),
                            jnp.bfloat16(0),
                        )
                        for code in own
                    ],
                    axis=0,
                )
                total_ref[book] += lax.dot_general(
                    left, right, (((1,), (1,)), ((), ())), preferred_element_type=jnp.float32
                )


def bin_grads(attended, misfit, codes, scales):
    groups, rows = codes.shape
    tokens = misfit.shape[0]
    block = math.gcd(groups, 32)
    chunk = math.gcd(rows, 512)
    total = pl.pallas_call(
        functools.partial(bin_kernel, chunk),
        grid=(groups // block,),
        in_specs=[
            pl.BlockSpec((block * GROUP, tokens), lambda g: (g, 0)),
            pl.BlockSpec((tokens, rows), lambda g: (0, 0)),
            pl.BlockSpec((block, rows), lambda g: (g, 0)),
            pl.BlockSpec((1, rows), lambda g: (0, 0)),
        ],
        out_specs=pl.BlockSpec(
            (2, LOW * OCTET * GROUP, OCTET * HIGH), lambda g: (0, 0, 0)
        ),
        out_shape=jax.ShapeDtypeStruct((2, LOW * OCTET * GROUP, OCTET * HIGH), jnp.float32),
        scratch_shapes=[pltpu.VMEM((block * GROUP, chunk), jnp.bfloat16)],
        compiler_params=pltpu.CompilerParams(vmem_limit_bytes=VMEM_LIMIT),
        cost_estimate=pl.CostEstimate(
            flops=4 * rows * groups * LOW * GROUP * OCTET * HIGH,
            bytes_accessed=rows * groups * 4,
            transcendentals=0,
        ),
        name="bin_grads",
    )(attended, misfit, codes, scales)
    split = total.reshape(2, LOW, OCTET, GROUP, OCTET, HIGH)
    same = jnp.eye(OCTET, dtype=jnp.float32)[None, None, :, None, :, None]
    kept = jnp.sum(split * same, axis=(2, 4))
    return kept.transpose(0, 3, 1, 2).reshape(2, ENTRIES, GROUP)


def attend(queries, key_rows, values):
    tok_rows, width = queries.shape
    heads_here = width // HEAD_DIM
    query_heads = queries.reshape(tok_rows, heads_here, HEAD_DIM)
    query_place = lax.axis_index("tok") * tok_rows + lax.iota(jnp.int32, tok_rows)
    key_piece = lax.all_gather(key_rows, "tok", axis=0, tiled=True)
    value_piece = lax.all_gather(values, "tok", axis=0, tiled=True)
    length = key_piece.shape[0]
    key_heads = key_piece.reshape(length, heads_here, HEAD_DIM)
    value_heads = value_piece.reshape(length, heads_here, HEAD_DIM)
    scores = jnp.einsum(
        "qhd,khd->hqk", query_heads, key_heads, preferred_element_type=jnp.float32
    ) / math.sqrt(HEAD_DIM)
    key_place = lax.iota(jnp.int32, length)
    allowed = (key_place[None, :] <= query_place[:, None])[None]
    peak = jnp.max(jnp.where(allowed, scores, -jnp.inf), axis=-1)
    exponent = jnp.where(allowed, jnp.exp(scores - peak[..., None]), 0.0)
    probs = exponent.astype(jnp.bfloat16)
    row_sum = jnp.sum(exponent, axis=-1)
    weighted = jnp.einsum("hqk,khd->hqd", probs, value_heads, preferred_element_type=jnp.float32)
    return (weighted / row_sum[..., None]).transpose(0, 2, 1).reshape(width, tok_rows).astype(
        jnp.bfloat16
    )


def local(
    queries, key_rows, values, code_first, code_second, book_first, book_second, scales, target
):
    books = jnp.stack([book_first.T, book_second.T]).astype(jnp.float32)
    weight, codes = dequantize(code_first, code_second, books, scales[None])
    attended = attend(queries, key_rows, values)
    head_cols = lax.all_gather(attended, "row", axis=0, tiled=True)
    gathered = lax.all_gather(head_cols, "tok", axis=1, tiled=True)
    partial_value = lax.dot_general(
        gathered, weight, (((0,), (0,)), ((), ())), preferred_element_type=jnp.float32
    )
    summed_out = lax.psum(partial_value, "col")
    misfit = (summed_out - target.astype(jnp.float32)).astype(jnp.bfloat16)
    tokens = misfit.shape[0]
    grad_scales = jnp.sum(misfit.astype(jnp.float32) * summed_out, axis=0) / (scales * tokens)
    grad_books = bin_grads(gathered, misfit, codes, (scales / tokens)[None])
    grad_books = lax.psum(grad_books, ("col", "row", "tok"))
    return (misfit, grad_scales, grad_books)


def solution(mesh):
    in_specs = (
        P("tok", ("col", "row")),
        P("tok", ("col", "row")),
        P("tok", ("col", "row")),
        P(("row", "tok"), "col"),
        P(("row", "tok"), "col"),
        P(),
        P(),
        P(("row", "tok")),
        P(None, ("row", "tok")),
    )
    out_specs = (P(None, ("row", "tok")), P(("row", "tok")), P())
    return jax.shard_map(local, mesh=mesh, in_specs=in_specs, out_specs=out_specs, check_vma=False)
```

time: 2330 us -> 397 us (0.17)
  matrix products: 1900 us -> 13.7 us
  local copies, waits for them, and re-layouts: 232 us -> 6.98 us
  Pallas kernels: 0 us -> 218 us
  loops' own time: 24.5 us -> 0 us
    dot_general x163 -> x3, matrix products: 1900 us -> 13.7 us  [the longest x1 12.3 us: local(): lax.dot_general(gathered, weight, (((0,), (0,)), ((), ())), preferred_ele...]
    pallas_call x0 -> x2, Pallas kernels: none -> 218 us  [the longest x1 115 us: bin_grads(): pl.pallas_call(functools.partial(bin_kernel, chunk), grid=(groups // bloc...]
    dynamic_update_slice x96 -> x0, local copies, waits for them, and re-layouts: 54.3 us -> none  [the longest x64 53.1 us: tile_unscaled(): lax.map(one_block, (code_first.reshape(count, block, groups), code_second...]
    dynamic_slice x64 -> x0, local copies, waits for them, and re-layouts: 50.6 us -> none  [the longest x32 31.8 us: step(): second_codes = lax.dynamic_slice_in_dim(code_second, start, block, 0)]
    add x32 -> x0, local copies, waits for them, and re-layouts: 36 us -> none  [dequantize(): return (first_part + second_part).reshape(rows, groups * GROUP)]
    reshape x33 -> x2, local copies, waits for them, and re-layouts: 37.9 us -> 2.57 us  [the longest x1 2.41 us: bin_grads(): split = total.reshape(2, LOW, OCTET, GROUP, OCTET, HIGH)]
    eq x32 -> x0, local copies, waits for them, and re-layouts: 31.5 us -> none  [one_hot_codes(): codes[..., None] == lax.iota(jnp.int32, ENTRIES)]
    another operation x2 -> x0, loops' own time: 24.5 us -> none  [the longest x1 23.9 us: tile_grads(): lax.scan(step, jnp.zeros((2, ENTRIES, GROUP), jnp.float32), lax.iota(jnp....]
  transfers between devices with their start and end apart: 3 -> 3, of which waited for: 2 -> 2; matrix products, arithmetic and copies ran while one was open for 36% -> 0% of each run, Pallas kernels for 0% -> 26%
where the time goes in v1:
time: 397 us
  Pallas kernels  218 us (55%)
  waiting for transfers between devices  80.3 us (20%)
  blocking collectives  57.8 us (15%)
  between operations  13.9 us (4%)
  matrix products  13.7 us (3%)
  local copies, waits for them, and re-layouts  6.98 us (2%)
  other arithmetic  6 us (2%)
    pallas_call x1, Pallas kernels, bin_grads(): pl.pallas_call(functools.partial(bin_kernel, chunk), grid=(groups // bloc...  115 us
    pallas_call x1, Pallas kernels, dequantize(): pl.pallas_call(dequantize_kernel, grid=(groups // LANES, rows // block),...  103 us
    psum x1, waiting for transfers between devices, local(): summed_out = lax.psum(partial_value, 'col')  51 us
    psum x1, blocking collectives, local(): grad_books = lax.psum(grad_books, ('col', 'row', 'tok'))  39.4 us
    all_gather x1, waiting for transfers between devices, local(): head_cols = lax.all_gather(attended, 'row', axis=0, tiled=True)  29.3 us
    dot_general x1, matrix products, local(): lax.dot_general(gathered, weight, (((0,), (0,)), ((), ())), preferred_ele...  12.3 us
    all_gather x1, blocking collectives, attend(): key_piece = lax.all_gather(key_rows, 'tok', axis=0, tiled=True)  9.95 us
    all_gather x1, blocking collectives, attend(): value_piece = lax.all_gather(values, 'tok', axis=0, tiled=True)  8.4 us
  transfers between devices with their start and end apart: 3, of which 2 were waited for; matrix products, arithmetic and copies ran while one was open for 0% of the time, Pallas kernels for 26%

profile of v1, /device:TPU:0, one launch (start us, length us, event | category | flops | bytes accessed | tf_op | source)
XLA Modules:
  0.0 396.7 jit_solution(13894450674379552386)
XLA Ops:
  7.2 0.0 copy-start
  7.2 0.0 all-gather.3.cloned.1.call-start
  7.2 1.1 copy.18
  8.4 10.0 %all_gather.12 = bf16[256,1024]{0,1:T(8,128)(2,1)S(1)} all-gather(bf16[128,1024]{0,1:T(8,128)(2,1)S(1)} %copy.18), channel_id=1, replica_groups=mesh['col'=4,'row'=4,'tok'=2] {'tok'}, dimensions={0}, use_global_device_ids=true | all-gather | bytes 786432 | tf_op jit(solution)/shard_map/all_gather | solution.py:172
  18.3 0.1 iota_compare_fusion
  18.4 8.4 %all_gather.13 = bf16[256,1024]{1,0:T(8,128)(2,1)S(1)} all-gather(bf16[128,1024]{1,0:T(8,128)(2,1)} %param.11), channel_id=1, replica_groups=mesh['col'=4,'row'=4,'tok'=2] {'tok'}, dimensions={0}, use_global_device_ids=true | all-gather | bytes 786432 | tf_op jit(solution)/shard_map/all_gather | solution.py:173
  26.8 0.2 copy.21
  27.1 0.3 convolution_multiply_fusion
  27.4 0.4 fusion.24
  27.8 0.0 copy-start.6
  27.8 0.0 copy-start.7
  27.8 1.1 fusion.9
  29.0 0.0 all-gather.3.cloned.1.call-update
  29.0 0.0 all-gather.5.cloned.1.call-start
  29.0 29.3 %all-gather.3.cloned.1.call-done = bf16[4096,128]{1,0:T(8,128)(2,1)} async-done(((bf16[1024,128]{1,0:T(8,128)(2,1)}), bf16[4096,128]{1,0:T(8,128)(2,1)}) %all-gather.3.cloned.1.call-update) | async-done | bytes 1048592 | tf_op jit(solution)/shard_map/all_gather | solution.py:198
  58.3 0.0 all-gather.5.cloned.1.call-update
  58.3 0.0 all-reduce.2.cloned.1.call-start
  58.4 102.8 %dequantize.1 = (bf16[4096,2048]{1,0:T(8,128)(2,1)}, s32[512,2048]{1,0:T(8,128)S(1)}) custom-call(s32[2048,512]{1,0:T(8,128)} %first_ref.1, s32[2048,512]{1,0:T(8,128)} %second_ref.1, f32[2,8,256]{2,1,0:T(8,128)S(1)} %maximum_convert_fusion.books_ref, f32[1,2048]{1,0:T(1,128)S(1)} %bitcast.29), custom_call_target="tpu_custom_call" | custom-call | flops 268435456 | bytes 29360128 | tf_op jit(solution)/shard_map/dequantize/pallas_call | solution.py:54
  161.2 1.9 copy-done.4
  163.1 12.3 %fusion.25 = f32[256,2048]{1,0:T(8,128)} fusion(bf16[4096,256]{1,0:T(8,128)(2,1)} %all-gather.5.cloned.1.call-done.attended_ref, bf16[4096,2048]{1,0:T(8,128)(2,1)} %get-tuple-element.5), kind=kOutput, calls=%fused_computation.28 | convolution fusion | flops 4294967296 | bytes 20971520 | tf_op jit(solution)/shard_map/dot_general | solution.py:200
  175.4 0.0 all-reduce.2.cloned.1.call-update
  175.4 51.0 %all-reduce.2.cloned.1.call-done = f32[256,2048]{1,0:T(8,128)} async-done(((f32[256,2048]{1,0:T(8,128)}), f32[256,2048]{1,0:T(8,128)}) %all-reduce.2.cloned.1.call-update) | async-done | bytes 2097168 | tf_op jit(solution)/shard_map/psum | solution.py:203
  226.4 2.0 multiply_reduce_fusion.1
  228.4 0.6 broadcast_multiply_fusion
  229.0 115.1 %bin_grads.1 = f32[2,512,256]{2,1,0:T(8,128)S(1)} custom-call(bf16[4096,256]{1,0:T(8,128)(2,1)S(1)} %copy-done.1, bf16[256,2048]{1,0:T(8,128)(2,1)S(1)} %get-tuple-element.8.misfit_ref, s32[512,2048]{1,0:T(8,128)} %copy-done.4, f32[1,2048]{1,0:T(1,128)S(1)} %bitcast.30), custom_call_target="tpu_custom_call" | custom-call | flops 68719476736 | bytes 4194304 | tf_op jit(solution)/shard_map/bin_grads/pallas_call | solution.py:139
  344.2 0.0 copy-start.2
  344.2 1.0 copy-done.2
  345.2 2.4 reshape.59
  347.6 2.9 multiply_reduce_fusion
  350.4 0.1 copy.22
  350.6 0.2 reshape.60
  350.7 39.4 %psum.15 = f32[2,256,8]{1,2,0:T(8,128)} all-reduce(f32[2,256,8]{1,2,0:T(8,128)S(1)} %reshape.60), channel_id=1, replica_groups=mesh['col'=4,'row'=4,'tok'=2] {'col','row','tok'}, use_global_device_ids=true, to_apply=%region_5.6 | all-reduce | flops 4096 | bytes 32768 | tf_op jit(solution)/shard_map/psum | solution.py:208
  (14 shorter events, 0.0 us)
Async XLA Ops:
  7.2 19.9 %copy-start = (bf16[128,1024]{1,0:T(8,128)(2,1)S(1)}, bf16[128,1024]{1,0:T(8,128)(2,1)}, u32[]{:S(2)}) copy-start(bf16[128,1024]{1,0:T(8,128)(2,1)} %param.9) | copy-start | bytes 786436
  7.2 51.1 %all-gather.3.cloned.1.call-start = ((), (), s32[]{:S(2)}) async-start(), calls=%async_computation | async-start | bytes 1310720 | tf_op jit(solution)/shard_map/all_gather | solution.py:198
  27.8 30.6 %copy-start.6 = (bf16[256,8]{0,1:T(8,128)(2,1)S(1)}, bf16[256,8]{0,1:T(8,128)(2,1)}, u32[]{:S(2)}) copy-start(bf16[256,8]{0,1:T(8,128)(2,1)} %param.15) | copy-start | bytes 12292
  27.8 30.6 %copy-start.7 = (bf16[256,8]{0,1:T(8,128)(2,1)S(1)}, bf16[256,8]{0,1:T(8,128)(2,1)}, u32[]{:S(2)}) copy-start(bf16[256,8]{0,1:T(8,128)(2,1)} %param.14) | copy-start | bytes 12292
  27.8 30.6 %copy-start.3 = (f32[2048]{0:T(1024)S(1)}, f32[2048]{0:T(1024)}, u32[]{:S(2)}) copy-start(f32[2048]{0:T(1024)} %param.16) | copy-start | bytes 24580
  29.0 134.1 %all-gather.5.cloned.1.call-start = ((), (), s32[]{:S(2)}) async-start(), calls=%async_computation.1 | async-start | bytes 3145728 | tf_op jit(solution)/shard_map/all_gather | solution.py:199
  58.3 168.1 %all-reduce.2.cloned.1.call-start = ((), (), s32[]{:S(2)}) async-start(), calls=%async_computation.2 | async-start | bytes 4194304 | tf_op jit(solution)/shard_map/psum | solution.py:203
  161.2 1.9 copy-start.4
  175.4 51.1 %copy-start.5 = (bf16[256,2048]{1,0:T(8,128)(2,1)S(1)}, bf16[256,2048]{1,0:T(8,128)(2,1)}, u32[]{:S(2)}) copy-start(bf16[256,2048]{1,0:T(8,128)(2,1)} %param.17) | copy-start | bytes 3145732
  175.4 53.6 %copy-start.1 = (bf16[4096,256]{1,0:T(8,128)(2,1)S(1)}, bf16[4096,256]{1,0:T(8,128)(2,1)}, u32[]{:S(2)}) copy-start(bf16[4096,256]{1,0:T(8,128)(2,1)} %all-gather.5.cloned.1.call-done.attended_ref) | copy-start | bytes 6291460
  344.2 1.0 copy-start.2
Sparse Core Ops, SparseCore 0:
  29.1 29.1 all-gather.2
  59.8 32.5 all-gather.4
  175.5 50.8 all-reduce.1

commit v2 on v1

--- a/solution.py
+++ b/solution.py
@@ -48,17 +48,19 @@
         weight_ref[rows16, :] = jnp.concatenate(parts, axis=0).astype(jnp.bfloat16)
 
 
-def dequantize(code_first, code_second, books, scales):
-    rows, groups = code_first.shape
+def dequantize(code_first, code_second, books, scales, part, parts):
+    groups = code_first.shape[1]
+    rows = code_first.shape[0] // parts
     block = math.gcd(rows, 512)
+    first = part * (rows // block)
     return pl.pallas_call(
         dequantize_kernel,
         grid=(groups // LANES, rows // block),
         in_specs=[
-            pl.BlockSpec((block, LANES), lambda g, o: (o, g)),
-            pl.BlockSpec((block, LANES), lambda g, o: (o, g)),
+            pl.BlockSpec((block, LANES), lambda g, o: (first + o, g)),
+            pl.BlockSpec((block, LANES), lambda g, o: (first + o, g)),
             pl.BlockSpec((2, GROUP, ENTRIES), lambda g, o: (0, 0, 0)),
-            pl.BlockSpec((1, block), lambda g, o: (0, o)),
+            pl.BlockSpec((1, block), lambda g, o: (0, first + o)),
         ],
         out_specs=[
             pl.BlockSpec((LANES * GROUP, block), lambda g, o: (g, o)),
@@ -136,7 +138,7 @@
     tokens = misfit.shape[0]
     block = math.gcd(groups, 32)
     chunk = math.gcd(rows, 512)
-    total = pl.pallas_call(
+    return pl.pallas_call(
         functools.partial(bin_kernel, chunk),
         grid=(groups // block,),
         in_specs=[
@@ -158,10 +160,87 @@
         ),
         name="bin_grads",
     )(attended, misfit, codes, scales)
-    split = total.reshape(2, LOW, OCTET, GROUP, OCTET, HIGH)
-    same = jnp.eye(OCTET, dtype=jnp.float32)[None, None, :, None, :, None]
-    kept = jnp.sum(split * same, axis=(2, 4))
-    return kept.transpose(0, 3, 1, 2).reshape(2, ENTRIES, GROUP)
+
+def fold_book(total):
+    groups_at = lax.broadcasted_iota(jnp.int32, total.shape, 0) // GROUP % OCTET
+    lanes_at = lax.broadcasted_iota(jnp.int32, total.shape, 1) // HIGH
+    kept = jnp.where(groups_at == lanes_at, total, 0.0)
+    kept = jnp.sum(kept.reshape(LOW, OCTET, GROUP, OCTET * HIGH), axis=1)
+    kept = kept.reshape(LOW * GROUP, OCTET * HIGH)
+    kept = kept[:, :LANES] + kept[:, LANES:]
+    kept = kept + pltpu.roll(kept, 2 * HIGH, 1)
+    return kept + pltpu.roll(kept, HIGH, 1)
+
+
+def sum_kernel(axes, *refs):
+    count = len(axes)
+    total_refs, out_ref = refs[: -3 * count - 1], refs[-3 * count - 1]
+    slots, sends, arrivals = (
+        refs[-3 * count : -2 * count],
+        refs[-2 * count : -count],
+        refs[-count:],
+    )
+    barrier = pltpu.get_barrier_semaphore()
+    peers = 0
+    for name, size in axes:
+        me = lax.axis_index(name)
+        for ahead in range(1, size):
+            pl.semaphore_signal(
+                barrier,
+                inc=1,
+                device_id={name: lax.rem(me + ahead, size)},
+                device_id_type=pl.DeviceIdType.MESH,
+            )
+            peers += 1
+    folded = []
+    for book in range(2):
+        total = total_refs[0][book]
+        for ref in total_refs[1:]:
+            total = total + ref[book]
+        folded.append(fold_book(total))
+    lane = lax.broadcasted_iota(jnp.int32, folded[0].shape, 1)
+    current = jnp.where(lane < HIGH, folded[0], folded[1])
+    pl.semaphore_wait(barrier, peers)
+    for stage, (name, size) in enumerate(axes):
+        me = lax.axis_index(name)
+        slots[stage][me] = current
+        copies = []
+        for ahead in range(1, size):
+            copy = pltpu.make_async_remote_copy(
+                src_ref=slots[stage].at[me],
+                dst_ref=slots[stage].at[me],
+                send_sem=sends[stage].at[ahead],
+                recv_sem=arrivals[stage].at[ahead],
+                device_id={name: lax.rem(me + ahead, size)},
+                device_id_type=pl.DeviceIdType.MESH,
+            )
+            copy.start()
+            copies.append(copy)
+        for copy in copies:
+            copy.wait()
+        current = slots[stage][0]
+        for place in range(1, size):
+            current = current + slots[stage][place]
+    out_ref[...] = current
+
+
+def sum_books(totals):
+    axes = [(name, lax.axis_size(name)) for name in ("col", "row", "tok")]
+    shape = (LOW * GROUP, LANES)
+    summed = pl.pallas_call(
+        functools.partial(sum_kernel, axes),
+        in_specs=[pl.BlockSpec(memory_space=pltpu.VMEM)] * len(totals),
+        out_specs=pl.BlockSpec(memory_space=pltpu.VMEM),
+        out_shape=jax.ShapeDtypeStruct(shape, jnp.float32),
+        scratch_shapes=[pltpu.VMEM((size, *shape), jnp.float32) for _, size in axes]
+        + [pltpu.SemaphoreType.DMA((size,)) for _, size in axes] * 2,
+        compiler_params=pltpu.CompilerParams(
+            collective_id=0, has_side_effects=True, vmem_limit_bytes=VMEM_LIMIT
+        ),
+        name="sum_books",
+    )(*totals)
+    split = summed[:, : 2 * HIGH].reshape(LOW, GROUP, 2, HIGH)
+    return split.transpose(2, 3, 0, 1).reshape(2, ENTRIES, GROUP)
 
 
 def attend(queries, key_rows, values):
@@ -192,21 +271,53 @@
 def local(
     queries, key_rows, values, code_first, code_second, book_first, book_second, scales, target
 ):
+    parts = 2
+    rows = scales.shape[0] // parts
     books = jnp.stack([book_first.T, book_second.T]).astype(jnp.float32)
-    weight, codes = dequantize(code_first, code_second, books, scales[None])
     attended = attend(queries, key_rows, values)
-    head_cols = lax.all_gather(attended, "row", axis=0, tiled=True)
-    gathered = lax.all_gather(head_cols, "tok", axis=1, tiled=True)
-    partial_value = lax.dot_general(
-        gathered, weight, (((0,), (0,)), ((), ())), preferred_element_type=jnp.float32
-    )
-    summed_out = lax.psum(partial_value, "col")
-    misfit = (summed_out - target.astype(jnp.float32)).astype(jnp.bfloat16)
-    tokens = misfit.shape[0]
-    grad_scales = jnp.sum(misfit.astype(jnp.float32) * summed_out, axis=0) / (scales * tokens)
-    grad_books = bin_grads(gathered, misfit, codes, (scales / tokens)[None])
-    grad_books = lax.psum(grad_books, ("col", "row", "tok"))
-    return (misfit, grad_scales, grad_books)
+    width, tok_rows = attended.shape
+    pieces = lax.all_gather(attended, ("row", "tok"), axis=0)
+    pieces = pieces.reshape(lax.axis_size("row"), lax.axis_size("tok"), width, tok_rows)
+    gathered = pieces.transpose(0, 2, 1, 3).reshape(pieces.shape[0] * width, -1)
+    tokens = gathered.shape[1]
+    misfits, grad_scales, totals = [], [], []
+
+    def finish(part, partial_value, codes, ahead):
+        here = slice(part * rows, (part + 1) * rows)
+        summed_out = lax.psum(partial_value, "col")
+        if totals:
+            wanted, totals[-1] = lax.optimization_barrier((target[:, here], totals[-1]))
+        else:
+            wanted = target[:, here]
+        misfit = (summed_out - wanted.astype(jnp.float32)).astype(jnp.bfloat16)
+        grad_scale = jnp.sum(misfit.astype(jnp.float32) * summed_out, axis=0)
+        grad_scales.append(grad_scale / (scales[here] * tokens))
+        next_value = None
+        if ahead is not None:
+            weight, misfit = lax.optimization_barrier((ahead, misfit))
+            next_value = project(weight)
+            misfit, next_value = lax.optimization_barrier((misfit, next_value))
+        misfits.append(misfit)
+        totals.append(bin_grads(gathered, misfit, codes, (scales[here] / tokens)[None]))
+        return next_value
+
+    def project(weight):
+        return lax.dot_general(
+            gathered, weight, (((0,), (0,)), ((), ())), preferred_element_type=jnp.float32
+        )
+
+    weight, codes = dequantize(code_first, code_second, books, scales[None], 0, parts)
+    partial_value = project(weight)
+    for part in range(parts):
+        ahead = next_codes = None
+        if part + 1 < parts:
+            row_scales, partial_value = lax.optimization_barrier((scales[None], partial_value))
+            ahead, next_codes = dequantize(
+                code_first, code_second, books, row_scales, part + 1, parts
+            )
+        partial_value = finish(part, partial_value, codes, ahead)
+        codes = next_codes
+    return (jnp.concatenate(misfits, axis=1), jnp.concatenate(grad_scales), sum_books(totals))
 
 
 def solution(mesh):

time: 397 us -> 302 us (0.76)
  waiting for transfers between devices: 80.3 us -> 0.05 us
  blocking collectives: 57.8 us -> 18.3 us
  Pallas kernels: 218 us -> 234 us
  local copies, waits for them, and re-layouts: 6.98 us -> 14.4 us
    psum x1 -> x2, waiting for transfers between devices: 51 us -> 0.01 us  [finish(): summed_out = lax.psum(partial_value, 'col')]
    psum x1 -> x0, blocking collectives: 39.4 us -> none  [local(): grad_books = lax.psum(grad_books, ('col', 'row', 'tok'))]
    all_gather x2 -> x1, waiting for transfers between devices: 29.3 us -> 0.01 us  [local(): pieces = lax.all_gather(attended, ('row', 'tok'), axis=0)]
    pallas_call x0 -> x1, Pallas kernels: none -> 14.5 us  [sum_books(): pl.pallas_call(functools.partial(sum_kernel, axes), in_specs=[pl.BlockSpe...]
    unnamed x17 -> x26, local copies, waits for them, and re-layouts: 4.07 us -> 8.67 us
    transpose x1, local copies, waits for them, and re-layouts: 0.13 us -> 4.5 us  [local(): gathered = pieces.transpose(0, 2, 1, 3).reshape(pieces.shape[0] * width, -1)]
    pallas_call x1 -> x2, Pallas kernels: 103 us -> 105 us  [dequantize(): pl.pallas_call(dequantize_kernel, grid=(groups // LANES, rows // block),...]
    dot_general x1 -> x2, matrix products: 12.3 us -> 13.4 us  [project(): lax.dot_general(gathered, weight, (((0,), (0,)), ((), ())), preferred_ele...]
  transfers between devices with their start and end apart: 3 -> 3, of which waited for: 2 -> 0; matrix products, arithmetic and copies ran while one was open for 0% -> 1% of each run, Pallas kernels for 26% -> 54%
where the time goes in v2:
time: 302 us; the launch traced here: 301 us
  Pallas kernels  234 us (77%)
  blocking collectives  18.3 us (6%)
  matrix products  14.9 us (5%)
  local copies, waits for them, and re-layouts  14.4 us (5%)
  between operations  14 us (5%)
  other arithmetic  5.47 us (2%)
    pallas_call x2, Pallas kernels, bin_grads(): pl.pallas_call(functools.partial(bin_kernel, chunk), grid=(groups // bloc...  115 us
    pallas_call x2, Pallas kernels, dequantize(): pl.pallas_call(dequantize_kernel, grid=(groups // LANES, rows // block),...  105 us
    pallas_call x1, Pallas kernels, sum_books(): pl.pallas_call(functools.partial(sum_kernel, axes), in_specs=[pl.BlockSpe...  14.5 us
    dot_general x2, matrix products, project(): lax.dot_general(gathered, weight, (((0,), (0,)), ((), ())), preferred_ele...  13.4 us
    all_gather x1, blocking collectives, attend(): key_piece = lax.all_gather(key_rows, 'tok', axis=0, tiled=True)  9.95 us
    unnamed x26, local copies, waits for them, and re-layouts  8.67 us
    all_gather x1, blocking collectives, attend(): value_piece = lax.all_gather(values, 'tok', axis=0, tiled=True)  8.4 us
  transfers between devices with their start and end apart: 3, of which 0 were waited for; matrix products, arithmetic and copies ran while one was open for 1% of the time, Pallas kernels for 54%

profile of v2, /device:TPU:0, one launch (start us, length us, event | category | flops | bytes accessed | tf_op | source)
XLA Modules:
  0.0 301.4 jit_solution(1317995976851912825)
XLA Ops:
  7.2 0.0 all-gather.2.cloned.1.call-start
  7.2 1.1 copy.21
  8.4 10.0 %all_gather.10 = bf16[256,1024]{0,1:T(8,128)(2,1)S(1)} all-gather(bf16[128,1024]{0,1:T(8,128)(2,1)S(1)} %copy.21), channel_id=1, replica_groups=mesh['col'=4,'row'=4,'tok'=2] {'tok'}, dimensions={0}, use_global_device_ids=true | all-gather | bytes 786432 | tf_op jit(solution)/shard_map/all_gather | solution.py:251
  18.3 0.1 iota_compare_fusion
  18.4 8.4 %all_gather.11 = bf16[256,1024]{1,0:T(8,128)(2,1)S(1)} all-gather(bf16[128,1024]{1,0:T(8,128)(2,1)} %param.11), channel_id=1, replica_groups=mesh['col'=4,'row'=4,'tok'=2] {'tok'}, dimensions={0}, use_global_device_ids=true | all-gather | bytes 786432 | tf_op jit(solution)/shard_map/all_gather | solution.py:252
  26.8 0.2 copy.24
  27.1 0.3 convolution_multiply_fusion
  27.4 0.4 fusion.25
  27.8 1.1 fusion.9
  29.0 0.0 all-reduce.3.cloned.1.call-start
  29.1 52.4 %dequantize.2 = (bf16[4096,1024]{1,0:T(8,128)(2,1)}, s32[512,1024]{1,0:T(8,128)S(1)}) custom-call(s32[2048,512]{1,0:T(8,128)} %first_ref.3, s32[2048,512]{1,0:T(8,128)} %second_ref.3, f32[2,8,256]{2,1,0:T(8,128)S(1)} %maximum_convert_fusion.books_ref, f32[1,2048]{1,0:T(1,128)S(1)} %bitcast.44), custom_call_target="tpu_custom_call" | custom-call | flops 134217728 | bytes 14680064 | tf_op jit(solution)/shard_map/dequantize/pallas_call | solution.py:56
  81.5 4.5 %copy.25 = bf16[4,1024,2,128]{3,2,1,0:T(2,128)(2,1)S(1)} copy(bf16[4,1024,2,128]{3,1,2,0:T(8,128)(2,1)} %bitcast.52) | data formatting | bytes 4194304 | tf_op jit(solution)/shard_map/transpose | solution.py:281
  86.0 1.3 copy-done.8
  87.3 6.7 %fusion.24 = f32[256,1024]{1,0:T(8,128)} fusion(bf16[4096,1024]{1,0:T(8,128)(2,1)} %get-tuple-element.15, bf16[512,8,2,128]{3,2,1,0:T(2,128)(2,1)S(1)} %bitcast.48), kind=kOutput, calls=%fused_computation.32 | convolution fusion | flops 2147483648 | bytes 11534336 | tf_op jit(solution)/shard_map/dot_general | solution.py:305
  94.1 0.2 all-reduce.5.cloned.1.call-start
  94.3 1.9 copy.37
  96.2 52.5 %dequantize.3 = (bf16[4096,1024]{1,0:T(8,128)(2,1)}, s32[512,1024]{1,0:T(8,128)S(1)}) custom-call(s32[2048,512]{1,0:T(8,128)} %first_ref.3, s32[2048,512]{1,0:T(8,128)} %second_ref.3, f32[2,8,256]{2,1,0:T(8,128)S(1)} %maximum_convert_fusion.books_ref, f32[1,2048]{1,0:T(1,128)S(1)} %bitcast.45), custom_call_target="tpu_custom_call" | custom-call | flops 134217728 | bytes 14680064 | tf_op jit(solution)/shard_map/dequantize/pallas_call | solution.py:56
  148.7 1.3 copy-done.6
  150.0 1.7 multiply_reduce_fusion.1
  151.7 0.4 copy-done.9
  152.1 6.7 %fusion.23 = f32[256,1024]{1,0:T(8,128)} fusion(bf16[4096,1024]{1,0:T(8,128)(2,1)} %get-tuple-element.20, bf16[512,8,2,128]{3,2,1,0:T(2,128)(2,1)S(1)} %bitcast.50), kind=kOutput, calls=%fused_computation.31 | convolution fusion | flops 2147483648 | bytes 11534336 | tf_op jit(solution)/shard_map/dot_general | solution.py:305
  158.8 1.6 copy-done.5
  160.4 57.2 %bin_grads.2.refs_0_ = f32[2,512,256]{2,1,0:T(8,128)S(1)} custom-call(bf16[4096,256]{1,0:T(8,128)(2,1)S(1)} %bitcast.41, bf16[256,1024]{1,0:T(8,128)(2,1)S(1)} %get-tuple-element.21.misfit_ref, s32[512,1024]{1,0:T(8,128)S(1)} %copy-done.5, f32[1,1024]{1,0:T(1,128)S(1)} %bitcast.47), custom_call_target="tpu_custom_call" | custom-call | flops 34359738368 | bytes 2097152 | tf_op jit(solution)/shard_map/bin_grads/pallas_call | solution.py:141
  217.7 1.0 copy-done.1
  218.7 1.6 multiply_reduce_fusion
  220.3 1.1 pad_maximum_fusion
  221.4 57.3 %bin_grads.3.refs_1_ = f32[2,512,256]{2,1,0:T(8,128)S(1)} custom-call(bf16[4096,256]{1,0:T(8,128)(2,1)S(1)} %bitcast.42, bf16[256,1024]{1,0:T(8,128)(2,1)S(1)} %get-tuple-element.30.misfit_ref, s32[512,1024]{1,0:T(8,128)S(1)} %copy-done.7, f32[1,1024]{1,0:T(1,128)S(1)} %bitcast.46), custom_call_target="tpu_custom_call" | custom-call | flops 34359738368 | bytes 2097152 | tf_op jit(solution)/shard_map/bin_grads/pallas_call | solution.py:141
  278.7 14.5 %sum_books.1 = f32[64,128]{1,0:T(8,128)S(1)} custom-call(f32[2,512,256]{2,1,0:T(8,128)S(1)} %copy-done.2, f32[2,512,256]{2,1,0:T(8,128)S(1)} %bin_grads.3.refs_1_), custom_call_target="tpu_custom_call" | custom-call | tf_op jit(solution)/shard_map/sum_books/pallas_call | solution.py:230
  293.3 0.1 reshape.69
  293.4 0.1 copy.26
  293.5 0.8 reshape.70
  294.3 0.6 pad_maximum_fusion.1
  (31 shorter events, 0.1 us)
Async XLA Ops:
  7.2 19.9 %copy-start = (bf16[128,1024]{1,0:T(8,128)(2,1)S(1)}, bf16[128,1024]{1,0:T(8,128)(2,1)}, u32[]{:S(2)}) copy-start(bf16[128,1024]{1,0:T(8,128)(2,1)} %param.9) | copy-start | bytes 786436
  7.2 74.3 %all-gather.2.cloned.1.call-start = ((), (), s32[]{:S(2)}) async-start(), calls=%async_computation | async-start | bytes 2359296 | tf_op jit(solution)/shard_map/all_gather | solution.py:279
  27.8 1.2 copy-start.10
  27.8 1.2 copy-start.11
  27.8 1.3 copy-start.3
  29.0 121.0 %all-reduce.3.cloned.1.call-start = ((), (), s32[]{:S(2)}) async-start(), calls=%async_computation.1 | async-start | bytes 2097152 | tf_op jit(solution)/shard_map/psum | solution.py:287
  81.5 4.5 %copy-start.4 = (s32[512,1024]{1,0:T(8,128)}, s32[512,1024]{1,0:T(8,128)S(1)}, u32[]{:S(2)}) copy-start(s32[512,1024]{1,0:T(8,128)S(1)} %get-tuple-element.23.codes_ref) | copy-start | bytes 6291460
  86.0 1.3 copy-start.8
  94.1 124.6 %all-reduce.5.cloned.1.call-start = ((), (), s32[]{:S(2)}) async-start(), calls=%async_computation.2 | async-start | bytes 2097152 | tf_op jit(solution)/shard_map/psum | solution.py:287
  148.7 1.3 copy-start.6
  150.0 2.1 copy-start.9
  158.8 1.6 copy-start.5
  160.4 58.3 %slice-start = ((bf16[256,2048]{1,0:T(8,128)(2,1)}), bf16[256,1024]{1,0:T(8,128)(2,1)S(1)}, s32[]{:S(2)}) async-start(bf16[256,2048]{1,0:T(8,128)(2,1)} %param.17), calls=%async_computation.3 | async-start | bytes 1048576 | tf_op jit(solution)/shard_map/slice | solution.py:289
  217.7 1.0 copy-start.1
  218.7 2.7 copy-start.7
  221.4 57.4 %copy-start.2 = (f32[2,512,256]{2,1,0:T(8,128)S(1)}, f32[2,512,256]{2,1,0:T(8,128)}, u32[]{:S(2)}) copy-start(f32[2,512,256]{2,1,0:T(8,128)} %copy-done.1) | copy-start | bytes 3145732
Sparse Core Ops, SparseCore 0:
  29.1 50.6 all-gather.1
  94.2 37.3 all-reduce.2
  159.0 37.3 all-reduce.4

commit v3 on v2

--- a/solution.py
+++ b/solution.py
@@ -33,7 +33,7 @@
         for book in range(2)
     ]
 
-    @pl.loop(0, groups // 2, unroll=4)
+    @pl.loop(0, groups // 2, unroll=16)
     def _(pair):
         parts = []
         for side in range(2):
@@ -99,7 +99,7 @@
             * scales_ref[:, cols]
         ).astype(jnp.bfloat16)
 
-        @pl.loop(0, groups // OCTET, unroll=2)
+        @pl.loop(0, groups // OCTET, unroll=groups // OCTET)
         def _(octet):
             grad = grad_ref[pl.ds(pl.multiple_of(octet * width, width), width), :]
             places = lax.broadcasted_iota(jnp.int32, (HIGH, chunk), 0).astype(jnp.bfloat16)
@@ -136,8 +136,8 @@
 def bin_grads(attended, misfit, codes, scales):
     groups, rows = codes.shape
     tokens = misfit.shape[0]
-    block = math.gcd(groups, 32)
-    chunk = math.gcd(rows, 512)
+    block = math.gcd(groups, 64)
+    chunk = math.gcd(rows, 1024)
     return pl.pallas_call(
         functools.partial(bin_kernel, chunk),
         grid=(groups // block,),

time: 302 us -> 253 us (0.84)
  Pallas kernels: 234 us -> 181 us
  waiting for transfers between devices: 0.05 us -> 4.7 us
    pallas_call x2, Pallas kernels: 115 us -> 76.5 us  [bin_grads(): pl.pallas_call(functools.partial(bin_kernel, chunk), grid=(groups // bloc...]
    pallas_call x2, Pallas kernels: 105 us -> 92.1 us  [dequantize(): pl.pallas_call(dequantize_kernel, grid=(groups // LANES, rows // block),...]
    all_gather x1, waiting for transfers between devices: 0.01 us -> 4.65 us  [local(): pieces = lax.all_gather(attended, ('row', 'tok'), axis=0)]
  transfers between devices with their start and end apart: 3 -> 3, of which waited for: 0 -> 1; matrix products, arithmetic and copies ran while one was open for 1% -> 1% of each run, Pallas kernels for 54% -> 52%
where the time goes in v3:
time: 253 us
  Pallas kernels  181 us (72%)
  blocking collectives  18.3 us (7%)
  matrix products  14.9 us (6%)
  between operations  14 us (6%)
  local copies, waits for them, and re-layouts  13.6 us (5%)
  other arithmetic  5.47 us (2%)
  waiting for transfers between devices  4.7 us (2%)
    pallas_call x2, Pallas kernels, dequantize(): pl.pallas_call(dequantize_kernel, grid=(groups // LANES, rows // block),...  92.1 us
    pallas_call x2, Pallas kernels, bin_grads(): pl.pallas_call(functools.partial(bin_kernel, chunk), grid=(groups // bloc...  76.5 us
    dot_general x2, matrix products, project(): lax.dot_general(gathered, weight, (((0,), (0,)), ((), ())), preferred_ele...  13.4 us
    pallas_call x1, Pallas kernels, sum_books(): pl.pallas_call(functools.partial(sum_kernel, axes), in_specs=[pl.BlockSpe...  12.9 us
    all_gather x1, blocking collectives, attend(): key_piece = lax.all_gather(key_rows, 'tok', axis=0, tiled=True)  9.95 us
    unnamed x26, local copies, waits for them, and re-layouts  8.67 us
    all_gather x1, blocking collectives, attend(): value_piece = lax.all_gather(values, 'tok', axis=0, tiled=True)  8.4 us
  transfers between devices with their start and end apart: 3, of which 1 were waited for; matrix products, arithmetic and copies ran while one was open for 1% of the time, Pallas kernels for 52%

profile of v3, /device:TPU:0, one launch (start us, length us, event | category | flops | bytes accessed | tf_op | source)
XLA Modules:
  0.0 252.6 jit_solution(6720023766859622067)
XLA Ops:
  7.2 1.1 copy.21
  8.4 10.0 %all_gather.10 = bf16[256,1024]{0,1:T(8,128)(2,1)S(1)} all-gather(bf16[128,1024]{0,1:T(8,128)(2,1)S(1)} %copy.21), channel_id=1, replica_groups=mesh['col'=4,'row'=4,'tok'=2] {'tok'}, dimensions={0}, use_global_device_ids=true | all-gather | bytes 786432 | tf_op jit(solution)/shard_map/all_gather | solution.py:251
  18.3 0.1 iota_compare_fusion
  18.4 8.4 %all_gather.11 = bf16[256,1024]{1,0:T(8,128)(2,1)S(1)} all-gather(bf16[128,1024]{1,0:T(8,128)(2,1)} %param.11), channel_id=1, replica_groups=mesh['col'=4,'row'=4,'tok'=2] {'tok'}, dimensions={0}, use_global_device_ids=true | all-gather | bytes 786432 | tf_op jit(solution)/shard_map/all_gather | solution.py:252
  26.8 0.2 copy.24
  27.1 0.3 convolution_multiply_fusion
  27.4 0.4 fusion.25
  27.8 1.1 fusion.9
  29.0 0.0 all-reduce.3.cloned.1.call-start
  29.1 45.9 %dequantize.2 = (bf16[4096,1024]{1,0:T(8,128)(2,1)}, s32[512,1024]{1,0:T(8,128)S(1)}) custom-call(s32[2048,512]{1,0:T(8,128)} %first_ref.3, s32[2048,512]{1,0:T(8,128)} %second_ref.3, f32[2,8,256]{2,1,0:T(8,128)S(1)} %maximum_convert_fusion.books_ref, f32[1,2048]{1,0:T(1,128)S(1)} %bitcast.44), custom_call_target="tpu_custom_call" | custom-call | flops 134217728 | bytes 14680064 | tf_op jit(solution)/shard_map/dequantize/pallas_call | solution.py:56
  75.0 4.7 %all-gather.2.cloned.1.call-done = bf16[8,1024,128]{2,1,0:T(8,128)(2,1)} async-done(((bf16[1,1024,128]{2,1,0:T(8,128)(2,1)}), bf16[8,1024,128]{2,1,0:T(8,128)(2,1)}) %all-gather.2.cloned.1.call-update) | async-done | bytes 2097168 | tf_op jit(solution)/shard_map/all_gather | solution.py:279
  79.6 3.7 %copy.25 = bf16[4,1024,2,128]{3,2,1,0:T(2,128)(2,1)S(1)} copy(bf16[4,1024,2,128]{3,1,2,0:T(8,128)(2,1)} %bitcast.52) | data formatting | bytes 4194304 | tf_op jit(solution)/shard_map/transpose | solution.py:281
  83.4 1.3 copy-done.8
  84.7 6.7 %fusion.24 = f32[256,1024]{1,0:T(8,128)} fusion(bf16[4096,1024]{1,0:T(8,128)(2,1)} %get-tuple-element.15, bf16[512,8,2,128]{3,2,1,0:T(2,128)(2,1)S(1)} %bitcast.48), kind=kOutput, calls=%fused_computation.32 | convolution fusion | flops 2147483648 | bytes 11534336 | tf_op jit(solution)/shard_map/dot_general | solution.py:305
  91.5 0.0 all-reduce.5.cloned.1.call-start
  91.5 1.9 copy.37
  93.4 46.2 %dequantize.3 = (bf16[4096,1024]{1,0:T(8,128)(2,1)}, s32[512,1024]{1,0:T(8,128)S(1)}) custom-call(s32[2048,512]{1,0:T(8,128)} %first_ref.3, s32[2048,512]{1,0:T(8,128)} %second_ref.3, f32[2,8,256]{2,1,0:T(8,128)S(1)} %maximum_convert_fusion.books_ref, f32[1,2048]{1,0:T(1,128)S(1)} %bitcast.45), custom_call_target="tpu_custom_call" | custom-call | flops 134217728 | bytes 14680064 | tf_op jit(solution)/shard_map/dequantize/pallas_call | solution.py:56
  139.6 1.3 copy-done.6
  140.9 1.7 multiply_reduce_fusion.1
  142.6 0.4 copy-done.9
  143.0 6.7 %fusion.23 = f32[256,1024]{1,0:T(8,128)} fusion(bf16[4096,1024]{1,0:T(8,128)(2,1)} %get-tuple-element.20, bf16[512,8,2,128]{3,2,1,0:T(2,128)(2,1)S(1)} %bitcast.50), kind=kOutput, calls=%fused_computation.31 | convolution fusion | flops 2147483648 | bytes 11534336 | tf_op jit(solution)/shard_map/dot_general | solution.py:305
  149.7 1.6 copy-done.5
  151.3 38.2 %bin_grads.2.refs_0_ = f32[2,512,256]{2,1,0:T(8,128)S(1)} custom-call(bf16[4096,256]{1,0:T(8,128)(2,1)S(1)} %bitcast.41, bf16[256,1024]{1,0:T(8,128)(2,1)S(1)} %get-tuple-element.21.misfit_ref, s32[512,1024]{1,0:T(8,128)S(1)} %copy-done.5, f32[1,1024]{1,0:T(1,128)S(1)} %bitcast.47), custom_call_target="tpu_custom_call" | custom-call | flops 34359738368 | bytes 2097152 | tf_op jit(solution)/shard_map/bin_grads/pallas_call | solution.py:141
  189.6 1.0 copy-done.1
  190.6 1.6 multiply_reduce_fusion
  192.2 1.1 pad_maximum_fusion
  193.3 38.3 %bin_grads.3.refs_1_ = f32[2,512,256]{2,1,0:T(8,128)S(1)} custom-call(bf16[4096,256]{1,0:T(8,128)(2,1)S(1)} %bitcast.42, bf16[256,1024]{1,0:T(8,128)(2,1)S(1)} %get-tuple-element.30.misfit_ref, s32[512,1024]{1,0:T(8,128)S(1)} %copy-done.7, f32[1,1024]{1,0:T(1,128)S(1)} %bitcast.46), custom_call_target="tpu_custom_call" | custom-call | flops 34359738368 | bytes 2097152 | tf_op jit(solution)/shard_map/bin_grads/pallas_call | solution.py:141
  231.5 12.9 %sum_books.1 = f32[64,128]{1,0:T(8,128)S(1)} custom-call(f32[2,512,256]{2,1,0:T(8,128)S(1)} %copy-done.2, f32[2,512,256]{2,1,0:T(8,128)S(1)} %bin_grads.3.refs_1_), custom_call_target="tpu_custom_call" | custom-call | tf_op jit(solution)/shard_map/sum_books/pallas_call | solution.py:230
  244.4 0.1 reshape.69
  244.5 0.1 copy.26
  244.7 0.8 reshape.70
  245.4 0.6 pad_maximum_fusion.1
  (31 shorter events, 0.2 us)
Async XLA Ops:
  7.2 19.9 %copy-start = (bf16[128,1024]{1,0:T(8,128)(2,1)S(1)}, bf16[128,1024]{1,0:T(8,128)(2,1)}, u32[]{:S(2)}) copy-start(bf16[128,1024]{1,0:T(8,128)(2,1)} %param.9) | copy-start | bytes 786436
  7.2 72.5 %all-gather.2.cloned.1.call-start = ((), (), s32[]{:S(2)}) async-start(), calls=%async_computation | async-start | bytes 2359296 | tf_op jit(solution)/shard_map/all_gather | solution.py:279
  27.8 1.2 copy-start.10
  27.8 1.2 copy-start.11
  27.8 1.3 copy-start.3
  29.0 111.9 %all-reduce.3.cloned.1.call-start = ((), (), s32[]{:S(2)}) async-start(), calls=%async_computation.1 | async-start | bytes 2097152 | tf_op jit(solution)/shard_map/psum | solution.py:287
  75.0 8.4 %copy-start.4 = (s32[512,1024]{1,0:T(8,128)}, s32[512,1024]{1,0:T(8,128)S(1)}, u32[]{:S(2)}) copy-start(s32[512,1024]{1,0:T(8,128)S(1)} %get-tuple-element.23.codes_ref) | copy-start | bytes 6291460
  83.4 1.3 copy-start.8
  91.5 99.1 %all-reduce.5.cloned.1.call-start = ((), (), s32[]{:S(2)}) async-start(), calls=%async_computation.2 | async-start | bytes 2097152 | tf_op jit(solution)/shard_map/psum | solution.py:287
  139.6 1.3 copy-start.6
  140.9 2.1 copy-start.9
  149.7 1.6 copy-start.5
  151.3 39.3 %slice-start = ((bf16[256,2048]{1,0:T(8,128)(2,1)}), bf16[256,1024]{1,0:T(8,128)(2,1)S(1)}, s32[]{:S(2)}) async-start(bf16[256,2048]{1,0:T(8,128)(2,1)} %param.17), calls=%async_computation.3 | async-start | bytes 1048576 | tf_op jit(solution)/shard_map/slice | solution.py:289
  189.6 1.0 copy-start.1
  190.6 2.7 %copy-start.7 = (s32[512,1024]{1,0:T(8,128)S(1)}, s32[512,1024]{1,0:T(8,128)}, u32[]{:S(2)}) copy-start(s32[512,1024]{1,0:T(8,128)} %copy-done.6) | copy-start | bytes 6291460
  193.3 38.3 %copy-start.2 = (f32[2,512,256]{2,1,0:T(8,128)S(1)}, f32[2,512,256]{2,1,0:T(8,128)}, u32[]{:S(2)}) copy-start(f32[2,512,256]{2,1,0:T(8,128)} %copy-done.1) | copy-start | bytes 3145732
Sparse Core Ops, SparseCore 0:
  29.1 50.5 all-gather.1
  91.6 34.5 all-reduce.2
  149.8 34.5 all-reduce.4
